TPU v7x, 512 devices: a whole 4x4x16 slice. The times are simulated.
512 devices in a mesh: img: 64 (over x, z_lo, core), blk: 8 (over z_hi, y).
Axes of the slice: x: 4, y: 4, z: 16 (z_hi: 2, z_lo: 8; z = z_hi * 8 + z_lo), core: 2. Of those that a mesh axis runs over, the one named last changes fastest.
Arguments:
- image_embeds: bfloat16 [6144, 1152], P(('img', 'blk')), may hold values from -48 to 48
- text_embeds: bfloat16 [6144, 1152], P(('img', 'blk')), may hold values from -48 to 48
- log_temp: float32 [1], replicated, may hold values from 1 to 2.3
- bias: float32 [1], replicated, may hold values from -3 to -1
Outputs:
- image_grads: float32 [6144, 1152], P(('img', 'blk'))
- text_grads: float32 [6144, 1152], P(('img', 'blk'))
All inputs are finite; a program needn't handle non-finite values.
Results may differ from a plain program's by a relative error of at most 0.00145.
Values may be sent and summed in bfloat16 or wider, within the bound.
No kernel may reach another device: no remote copies, remote signals or barrier semaphores. Data moves between devices by JAX's collectives and lax.ppermute only.
A program may use at most 64 MiB of HBM per device.

v0:
```python
import jax
import jax.numpy as jnp
from jax import lax
from jax.experimental import pallas as pl
from jax.experimental.pallas import tpu as pltpu
from jax.sharding import Mesh, PartitionSpec as P

EPS = 1e-06
AXES = ("x", "zm", "zn", "core", "zh", "y")
SIZES = (4, 2, 4, 2, 2, 4)
PLANE = ("x", "core", "y")
LINE = ("zm", "zn", "zh")
FAR = ("zm", "zh")
VMEM = 48 * 1024 * 1024

ROWS = 12
WIDTH = 1152
TALL = 16
MAIN = 896
REST = WIDTH - MAIN
STEP = TALL - ROWS
PIECES = [
    (
        slice(m * STEP, (m + 1) * STEP),
        slice(g * 128, (g + 1) * 128),
        slice((3 * g + m) * 128, (3 * g + m + 1) * 128),
    )
    for g in range(REST // 128)
    for m in range(ROWS // STEP)
]

WIDE = 1024


def spread_kernel(emb_ref, out_ref, unit_ref, inverse_ref, half_ref, block):
    wide = emb_ref[...].astype(jnp.float32)
    inverse = lax.rsqrt(jnp.sum(wide * wide, axis=1, keepdims=True) + EPS)
    unit_ref[...] = wide * inverse
    inverse_ref[...] = inverse
    half_ref[...] = unit_ref[...].astype(jnp.bfloat16)
    block[:ROWS, :] = unit_ref[:, :MAIN]
    block[ROWS:, :] = jnp.zeros((STEP, MAIN), jnp.float32)
    for rows, cols, place in PIECES:
        block[ROWS:, place] = unit_ref[rows, MAIN + cols.start : MAIN + cols.stop]
    out_ref[...] = jnp.broadcast_to(block[...].astype(jnp.bfloat16)[None], out_ref.shape)


def spread(emb, peers):
    return pl.pallas_call(
        spread_kernel,
        out_shape=[
            jax.ShapeDtypeStruct((peers, TALL, MAIN), jnp.bfloat16),
            jax.ShapeDtypeStruct(emb.shape, jnp.float32),
            jax.ShapeDtypeStruct((ROWS, 1), jnp.float32),
            jax.ShapeDtypeStruct(emb.shape, jnp.bfloat16),
        ],
        scratch_shapes=[pltpu.VMEM((TALL, MAIN), jnp.float32)],
        compiler_params=pltpu.CompilerParams(vmem_limit_bytes=VMEM),
        cost_estimate=pl.CostEstimate(flops=100_000, bytes_accessed=1_000_000, transcendentals=0),
    )(emb)


def packed(main, rest, n):
    for rows, cols, place in PIECES:
        main[:n, ROWS:, place] = rest[:n, rows, cols]
    return main[:n]


def text_kernel(temp_ref, bias_ref, place_ref, images_ref, *refs):
    text_refs = refs[:4]
    coeff_ref, texts = refs[4:6]
    outs = refs[6:10]
    images, rest, main = refs[10:]
    rest[:, ROWS:, :] = jnp.zeros((rest.shape[0], STEP, REST), jnp.float32)
    first = [0]
    for ref in text_refs:
        first.append(first[-1] + ref.shape[0])
    groups = [(images, 0, images_ref)] + [(texts, i, ref) for i, ref in zip(first, text_refs)]
    for whole, start, ref in groups:
        n = ref.shape[0]
        span = pl.ds(start * TALL, n * TALL)
        whole[span, :MAIN] = ref[...].reshape(n * TALL, MAIN)
        for rows, cols, place in PIECES:
            rest[:n, rows, cols] = ref[:, ROWS:, place].astype(jnp.float32)
        whole[span, MAIN:] = rest[:n].reshape(n * TALL, REST).astype(jnp.bfloat16)

    scale = jnp.exp(jnp.full((1, 1), temp_ref[0], jnp.float32))
    logits = (
        scale
        * lax.dot_general(
            images[...], texts[...], (((1,), (1,)), ((), ())), preferred_element_type=jnp.float32
        )
        + bias_ref[0]
    )
    row = lax.broadcasted_iota(jnp.int32, logits.shape, 0)
    col = lax.broadcasted_iota(jnp.int32, logits.shape, 1)
    row_in, col_in = row % TALL, col % TALL
    real = (row_in < ROWS) & (col_in < ROWS)
    same = (row - place_ref[0] * TALL == row_in) & (col - place_ref[1] * TALL == col_in)
    same = same & (row_in == col_in)
    sig = jax.nn.sigmoid(jnp.where(same, -logits, logits))
    coeff = jnp.where(real, jnp.where(same, -sig, sig) * scale, 0.0).astype(jnp.bfloat16)
    coeff_ref[...] = coeff

    n = first[-1]
    flip = (((0,), (0,)), ((), ()))
    main[...] = lax.dot_general(
        coeff, images[:, :MAIN], flip, preferred_element_type=jnp.float32
    ).reshape(n, TALL, MAIN)
    rest[:n] = lax.dot_general(
        coeff, images[:, MAIN:], flip, preferred_element_type=jnp.float32
    ).reshape(n, TALL, REST)
    packed(main, rest, n)
    for start, out in zip(first, outs):
        out[...] = main[start : start + out.shape[0]].astype(out.dtype)


def text_terms(log_temp, bias, place, images, texts):
    n_images, n_texts = images.shape[0], sum(text.shape[0] for text in texts)
    return pl.pallas_call(
        text_kernel,
        in_specs=[pl.BlockSpec(memory_space=pltpu.SMEM)] * 3
        + [pl.BlockSpec(memory_space=pltpu.VMEM)] * (1 + len(texts)),
        out_shape=[
            jax.ShapeDtypeStruct((n_images * TALL, n_texts * TALL), jnp.bfloat16),
            jax.ShapeDtypeStruct((n_texts * TALL, WIDTH), jnp.bfloat16),
            jax.ShapeDtypeStruct(texts[0].shape, jnp.float32),
        ]
        + [jax.ShapeDtypeStruct(text.shape, jnp.bfloat16) for text in texts[1:]],
        scratch_shapes=[
            pltpu.VMEM((n_images * TALL, WIDTH), jnp.bfloat16),
            pltpu.VMEM((n_images, TALL, REST), jnp.float32),
            pltpu.VMEM((n_texts, TALL, MAIN), jnp.float32),
        ],
        compiler_params=pltpu.CompilerParams(vmem_limit_bytes=VMEM),
        cost_estimate=pl.CostEstimate(
            flops=600_000_000, bytes_accessed=4_000_000, transcendentals=131_072
        ),
    )(log_temp, bias, place, images, *texts)


def image_kernel(coeff_ref, texts_ref, out_ref, rest, main):
    n = out_ref.shape[0]
    coeff = coeff_ref[...]
    main[...] = jnp.dot(
        coeff, texts_ref[:, :MAIN], preferred_element_type=jnp.float32
    ).reshape(n, TALL, MAIN)
    rest[...] = jnp.dot(
        coeff, texts_ref[:, MAIN:], preferred_element_type=jnp.float32
    ).reshape(n, TALL, REST)
    out_ref[...] = packed(main, rest, n).astype(jnp.bfloat16)


def image_terms(coeff, texts):
    n = coeff.shape[0] // TALL
    return pl.pallas_call(
        image_kernel,
        out_shape=jax.ShapeDtypeStruct((n, TALL, MAIN), jnp.bfloat16),
        scratch_shapes=[
            pltpu.VMEM((n, TALL, REST), jnp.float32),
            pltpu.VMEM((n, TALL, MAIN), jnp.float32),
        ],
        compiler_params=pltpu.CompilerParams(vmem_limit_bytes=VMEM),
        cost_estimate=pl.CostEstimate(
            flops=300_000_000, bytes_accessed=2_000_000, transcendentals=0
        ),
    )(coeff, texts)


def rounded(value):
    return value.astype(jnp.bfloat16)


def far_kernel(own_ref, near_a, near_b, near_c, half_ref, out_ref, block):
    n = own_ref.shape[0]
    part = own_ref[...] + sum(ref[...].astype(jnp.float32) for ref in (near_a, near_b, near_c))
    block[:, :ROWS, :MAIN] = part[:, :ROWS]
    block[:, ROWS:, :] = jnp.zeros((n, STEP, WIDTH), jnp.float32)
    for rows, cols, place in PIECES:
        block[:, rows, MAIN + cols.start : MAIN + cols.stop] = part[:, ROWS:, place]
    half = half_ref[: n * TALL, :].astype(jnp.float32).reshape(n, TALL, WIDTH)

    along = jnp.sum(block[...] * half, axis=2, keepdims=True)
    lane = lax.broadcasted_iota(jnp.int32, (n, STEP, 128), 2)
    spare = slice(6 * 128, 7 * 128)

    def store(factor, first):
        held = out_ref[:, ROWS:, spare]
        for m in range(ROWS // STEP):
            piece = rounded(jnp.broadcast_to(factor[:, m * STEP : (m + 1) * STEP], lane.shape))
            held = jnp.where(lane == first + m, piece, held)
        out_ref[:, ROWS:, spare] = held

    def load(first):
        held = out_ref[:, ROWS:, spare].astype(jnp.float32)
        return [
            jnp.sum(jnp.where(lane == first + m, held, 0.0), axis=2, keepdims=True)
            for m in range(ROWS // STEP)
        ]

    out_ref[:, ROWS:, :] = jnp.zeros((n, STEP, WIDE), jnp.bfloat16)
    store(along, 0)
    for m, factor in enumerate(load(0)):
        rows = slice(m * STEP, (m + 1) * STEP)
        block[:, rows, :] = block[:, rows, :] - factor * half[:, rows]
    mean = jnp.sum(block[...], axis=1, keepdims=True) * (1.0 / ROWS)
    mean = rounded(mean).astype(jnp.float32)
    size = jnp.sum(mean * mean, axis=2, keepdims=True)
    along = jnp.sum(block[...] * mean, axis=2, keepdims=True)
    store(jnp.where(size > 0.0, along / jnp.where(size > 0.0, size, 1.0), 0.0), 4)
    for j in range(WIDTH // 128):
        row = ROWS + j % STEP
        cols = slice((3 + j // STEP) * 128, (4 + j // STEP) * 128)
        out_ref[:, row : row + 1, cols] = rounded(mean[:, :, j * 128 : (j + 1) * 128])
    for m, factor in enumerate(load(4)):
        rows = slice(m * STEP, (m + 1) * STEP)
        left = block[:, rows, :] - factor * mean
        block[:, rows, :] = left
    out_ref[:, :ROWS, :] = rounded(block[:, :ROWS, :WIDE])
    for m in range(ROWS // STEP):
        rows = slice(m * STEP, (m + 1) * STEP)
        out_ref[:, ROWS:, m * 128 : (m + 1) * 128] = rounded(block[:, rows, WIDE:])


def far_message(own, near, half):
    n = own.shape[0]
    return pl.pallas_call(
        far_kernel,
        out_shape=jax.ShapeDtypeStruct((n, TALL, WIDE), jnp.bfloat16),
        scratch_shapes=[pltpu.VMEM((n, TALL, WIDTH), jnp.float32)],
        compiler_params=pltpu.CompilerParams(vmem_limit_bytes=VMEM),
        cost_estimate=pl.CostEstimate(flops=500_000, bytes_accessed=1_000_000, transcendentals=0),
    )(own, *near, half)


def project(direction, unit, inverse):
    along = jnp.sum(unit * direction, axis=1, keepdims=True)
    return (direction - unit * along) * inverse


def finish_images_kernel(unit_ref, inverse_ref, back_ref, out_ref, block):
    total = jnp.sum(back_ref[...].astype(jnp.float32), axis=0)
    block[:, :MAIN] = total[:ROWS]
    for rows, cols, place in PIECES:
        block[rows, MAIN + cols.start : MAIN + cols.stop] = total[ROWS:, place]
    out_ref[...] = project(block[...], unit_ref[...], inverse_ref[...])


def finish_texts_kernel(unit_ref, inverse_ref, half_ref, back_ref, out_ref, block):
    back = back_ref[...].astype(jnp.float32)
    total = jnp.sum(back, axis=0)
    block[:, :WIDE] = total[:ROWS]
    spare = back[:, ROWS:, 6 * 128 : 7 * 128]
    lane = lax.broadcasted_iota(jnp.int32, spare.shape, 2)
    means = [
        back[:, ROWS + j % STEP : ROWS + j % STEP + 1, (3 + j // STEP) * 128 : (4 + j // STEP) * 128]
        for j in range(WIDTH // 128)
    ]
    for m in range(ROWS // STEP):
        rows = slice(m * STEP, (m + 1) * STEP)
        block[rows, WIDE:] = total[ROWS:, m * 128 : (m + 1) * 128]
        own = jnp.sum(jnp.where(lane == m, spare, 0.0), axis=2, keepdims=True)
        mean = jnp.sum(jnp.where(lane == 4 + m, spare, 0.0), axis=2, keepdims=True)
        block[rows, :] += jnp.sum(own, axis=0) * half_ref[rows, :].astype(jnp.float32)
        for j, piece in enumerate(means):
            block[rows, j * 128 : (j + 1) * 128] += jnp.sum(mean * piece, axis=0)
    out_ref[...] = project(block[...], unit_ref[...], inverse_ref[...])


def finish(kernel, unit, *operands):
    return pl.pallas_call(
        kernel,
        out_shape=jax.ShapeDtypeStruct(unit.shape, jnp.float32),
        scratch_shapes=[pltpu.VMEM((ROWS, WIDTH), jnp.float32)],
        compiler_params=pltpu.CompilerParams(vmem_limit_bytes=VMEM),
        cost_estimate=pl.CostEstimate(flops=500_000, bytes_accessed=1_000_000, transcendentals=0),
    )(unit, *operands)


def along_z(value, move):
    def spot(z):
        return (z // 4 % 2) * 8 + (z % 4) * 2 + z // 8

    return lax.ppermute(value, LINE, [(spot(z), spot(move(z) % 16)) for z in range(16)])


NEAR = (
    (lambda z: z + 1, lambda z: z - 1),
    (lambda z: z - 1, lambda z: z + 1),
    (lambda z: z + 2 - 4 * (z % 2), lambda z: z + 2 - 4 * (z % 2)),
)


def on_device(image_embeds, text_embeds, log_temp, bias):
    place = jnp.stack([lax.axis_index(PLANE), lax.axis_index(FAR)]).astype(jnp.int32)

    own, txt_unit, txt_inv, txt_half = spread(text_embeds, lax.axis_size(FAR))
    own = lax.all_to_all(own, FAR, 0, 0)
    sent, img_unit, img_inv, _ = spread(image_embeds, lax.axis_size(PLANE))
    sent, own = lax.optimization_barrier((sent, own))
    images = lax.all_to_all(sent, PLANE, 0, 0)
    texts = [own] + [along_z(own, there) for there, _ in NEAR]

    coeff, whole, part, *near_parts = text_terms(log_temp, bias, place, images, texts)
    image_back = lax.all_to_all(image_terms(coeff, whole), PLANE, 0, 0)
    near = [along_z(near_part, home) for near_part, (_, home) in zip(near_parts, NEAR)]
    message, image_back = lax.optimization_barrier((far_message(part, near, whole), image_back))
    text_back = lax.all_to_all(message, FAR, 0, 0)
    return (
        finish(finish_images_kernel, img_unit, img_inv, image_back),
        finish(finish_texts_kernel, txt_unit, txt_inv, txt_half, text_back),
    )


def solution(mesh):
    fine = Mesh(mesh.devices.reshape(SIZES), AXES)
    split = P(AXES, None)
    return jax.shard_map(
        on_device,
        mesh=fine,
        in_specs=(split, split, P(), P()),
        out_specs=(split, split),
        check_vma=False,
    )
```

profile of v0, /device:TPU:32, one launch (start us, length us, event | category | flops | bytes accessed | tf_op | source)
XLA Modules:
  0.0 101.4 jit_solution(14584188252605754403)
XLA Ops:
  0.6 0.0 copy-start
  0.6 0.8 copy-done
  1.4 0.8 shard_map.60
  2.2 0.0 copy-start.1
  2.2 14.3 %all-to-all-start = ((bf16[4,16,896]{2,1,0:T(8,128)(2,1)}), bf16[4,16,896]{2,1,0:T(8,128)(2,1)S(1)}, u32[]{:S(2)}, u32[]{:S(2)}) async-start(bf16[4,16,896]{2,1,0:T(8,128)(2,1)} %get-tuple-element.22), calls=%async_computation | async-start | bytes 229376 | tf_op jit(solution)/shard_map/all_to_all | solution.py:298
  16.5 0.0 copy-done.1
  16.5 1.1 %shard_map.59 = (bf16[32,16,896]{2,1,0:T(8,128)(2,1)}, f32[12,1152]{1,0:T(8,128)S(1)}, f32[12,1]{1,0:T(8,128)S(1)}, bf16[12,1152]{1,0:T(8,128)(2,1)}) custom-call(bf16[12,1152]{1,0:T(8,128)(2,1)S(1)} %copy-done.1), custom_call_target="tpu_custom_call" | custom-call | flops 100000 | bytes 1000000 | tf_op jit(solution)/shard_map/pallas_call | solution.py:49
  17.6 14.6 %all-to-all-done.refs_0_ = bf16[4,16,896]{2,1,0:T(8,128)(2,1)S(1)} async-done(((bf16[4,16,896]{2,1,0:T(8,128)(2,1)}), bf16[4,16,896]{2,1,0:T(8,128)(2,1)S(1)}, u32[]{:S(2)}, u32[]{:S(2)}) %all-to-all-start) | async-done | bytes 114720 | tf_op jit(solution)/shard_map/all_to_all | solution.py:298
  32.2 7.3 %all-to-all-start.1 = ((bf16[32,16,896]{2,1,0:T(8,128)(2,1)}), bf16[32,16,896]{2,1,0:T(8,128)(2,1)S(1)}, u32[]{:S(2)}, u32[]{:S(2)}) async-start(bf16[32,16,896]{2,1,0:T(8,128)(2,1)} %get-tuple-element.23), calls=%async_computation.1 | async-start | bytes 1835008 | tf_op jit(solution)/shard_map/all_to_all | solution.py:301
  39.5 1.9 %collective-permute-start.2 = (bf16[4,16,896]{2,1,0:T(8,128)(2,1)S(1)}, bf16[4,16,896]{2,1,0:T(8,128)(2,1)S(1)}, u32[]{:S(2)}, u32[]{:S(2)}) collective-permute-start(bf16[4,16,896]{2,1,0:T(8,128)(2,1)S(1)} %all-to-all-done.refs_0_), channel_id=1, source_target_pairs={{0,32},{16,116},{32,64},{48,16},{64,96},{80,48},{96,4},{112,80},{4... | collective-permute-start | bytes 344072 | tf_op jit(solution)/shard_map/ppermute | solution.py:284
  41.5 3.8 %collective-permute-start.1 = (bf16[4,16,896]{2,1,0:T(8,128)(2,1)S(1)}, bf16[4,16,896]{2,1,0:T(8,128)(2,1)S(1)}, u32[]{:S(2)}, u32[]{:S(2)}) collective-permute-start(bf16[4,16,896]{2,1,0:T(8,128)(2,1)S(1)} %all-to-all-done.refs_0_), channel_id=1, source_target_pairs={{0,116},{16,0},{32,16},{48,32},{64,48},{80,64},{96,80},{112,96},{4... | collective-permute-start | bytes 344072 | tf_op jit(solution)/shard_map/ppermute | solution.py:284
  45.2 2.1 %collective-permute-start = (bf16[4,16,896]{2,1,0:T(8,128)(2,1)S(1)}, bf16[4,16,896]{2,1,0:T(8,128)(2,1)S(1)}, u32[]{:S(2)}, u32[]{:S(2)}) collective-permute-start(bf16[4,16,896]{2,1,0:T(8,128)(2,1)S(1)} %all-to-all-done.refs_0_), channel_id=1, source_target_pairs={{0,16},{16,32},{32,48},{48,64},{64,80},{80,96},{96,112},{112,4},{4... | collective-permute-start | bytes 344072 | tf_op jit(solution)/shard_map/ppermute | solution.py:284
  48.6 0.1 pad_add_fusion.place_ref
  48.7 0.0 collective-permute-done.2.refs_3_
  48.7 1.4 %collective-permute-done.1.refs_2_ = bf16[4,16,896]{2,1,0:T(8,128)(2,1)S(1)} collective-permute-done((bf16[4,16,896]{2,1,0:T(8,128)(2,1)S(1)}, bf16[4,16,896]{2,1,0:T(8,128)(2,1)S(1)}, u32[]{:S(2)}, u32[]{:S(2)}) %collective-permute-start.1) | collective-permute-done | bytes 114720 | tf_op jit(solution)/shard_map/ppermute | solution.py:284
  50.1 1.8 %collective-permute-done.refs_1_ = bf16[4,16,896]{2,1,0:T(8,128)(2,1)S(1)} collective-permute-done((bf16[4,16,896]{2,1,0:T(8,128)(2,1)S(1)}, bf16[4,16,896]{2,1,0:T(8,128)(2,1)S(1)}, u32[]{:S(2)}, u32[]{:S(2)}) %collective-permute-start) | collective-permute-done | bytes 114720 | tf_op jit(solution)/shard_map/ppermute | solution.py:284
  51.9 3.3 %all-to-all-done.1.images_ref = bf16[32,16,896]{2,1,0:T(8,128)(2,1)S(1)} async-done(((bf16[32,16,896]{2,1,0:T(8,128)(2,1)}), bf16[32,16,896]{2,1,0:T(8,128)(2,1)S(1)}, u32[]{:S(2)}, u32[]{:S(2)}) %all-to-all-start.1) | async-done | bytes 917536 | tf_op jit(solution)/shard_map/all_to_all | solution.py:301
  55.2 2.4 %shard_map.61 = (bf16[512,256]{1,0:T(8,128)(2,1)S(1)}, bf16[256,1152]{1,0:T(8,128)(2,1)S(1)}, f32[4,16,896]{2,1,0:T(8,128)S(1)}, bf16[4,16,896]{2,1,0:T(8,128)(2...) custom-call(f32[1]{0:T(128)S(6)} %copy.6.temp_ref, f32[1]{0:T(128)S(6)} %copy.7.bias_ref, ...), custom_call_target="tpu_custom_call" | custom-call | flops 600000000 | bytes 4000000 | tf_op jit(solution)/shard_map/pallas_call | solution.py:120
  57.7 1.5 %shard_map.63 = bf16[32,16,896]{2,1,0:T(8,128)(2,1)} custom-call(bf16[512,256]{1,0:T(8,128)(2,1)S(1)} %get-tuple-element.30.coeff_ref, bf16[256,1152]{1,0:T(8,128)(2,1)S(1)} %get-tuple-element.29.half_ref.texts_ref), custom_call_target="tpu_custom_call" | custom-call | flops 300000000 | bytes 2000000 | tf_op jit(solution)/shard_map/pallas_call | solution.py:156
  59.2 4.0 %all-to-all-start.2 = ((bf16[32,16,896]{2,1,0:T(8,128)(2,1)}), bf16[32,16,896]{2,1,0:T(8,128)(2,1)S(1)}, u32[]{:S(2)}, u32[]{:S(2)}) async-start(bf16[32,16,896]{2,1,0:T(8,128)(2,1)} %shard_map.63), calls=%async_computation.2 | async-start | bytes 1835008 | tf_op jit(solution)/shard_map/all_to_all | solution.py:305
  63.3 3.3 %collective-permute-start.3 = (bf16[4,16,896]{2,1,0:T(8,128)(2,1)S(1)}, bf16[4,16,896]{2,1,0:T(8,128)(2,1)S(1)}, u32[]{:S(2)}, u32[]{:S(2)}) collective-permute-start(bf16[4,16,896]{2,1,0:T(8,128)(2,1)S(1)} %get-tuple-element.26), channel_id=1, source_target_pairs={{0,116},{16,0},{32,16},{48,32},{64,48},{80,64},{96,80},{112,96},{4... | collective-permute-start | bytes 344072 | tf_op jit(solution)/shard_map/ppermute | solution.py:284
  66.5 2.6 %collective-permute-start.4 = (bf16[4,16,896]{2,1,0:T(8,128)(2,1)S(1)}, bf16[4,16,896]{2,1,0:T(8,128)(2,1)S(1)}, u32[]{:S(2)}, u32[]{:S(2)}) collective-permute-start(bf16[4,16,896]{2,1,0:T(8,128)(2,1)S(1)} %get-tuple-element.27), channel_id=1, source_target_pairs={{0,16},{16,32},{32,48},{48,64},{64,80},{80,96},{96,112},{112,4},{4... | collective-permute-start | bytes 344072 | tf_op jit(solution)/shard_map/ppermute | solution.py:284
  69.1 4.4 %collective-permute-start.5 = (bf16[4,16,896]{2,1,0:T(8,128)(2,1)S(1)}, bf16[4,16,896]{2,1,0:T(8,128)(2,1)S(1)}, u32[]{:S(2)}, u32[]{:S(2)}) collective-permute-start(bf16[4,16,896]{2,1,0:T(8,128)(2,1)S(1)} %get-tuple-element.28), channel_id=1, source_target_pairs={{0,32},{16,116},{32,64},{48,16},{64,96},{80,48},{96,4},{112,80},{4... | collective-permute-start | bytes 344072 | tf_op jit(solution)/shard_map/ppermute | solution.py:284
  73.6 0.0 collective-permute-done.3.near_a
  73.6 0.0 collective-permute-done.4.near_b
  73.6 4.2 %collective-permute-done.5.near_c = bf16[4,16,896]{2,1,0:T(8,128)(2,1)S(1)} collective-permute-done((bf16[4,16,896]{2,1,0:T(8,128)(2,1)S(1)}, bf16[4,16,896]{2,1,0:T(8,128)(2,1)S(1)}, u32[]{:S(2)}, u32[]{:S(2)}) %collective-permute-start.5) | collective-permute-done | bytes 114720 | tf_op jit(solution)/shard_map/ppermute | solution.py:284
  77.8 1.3 %shard_map.62 = bf16[4,16,1024]{2,1,0:T(8,128)(2,1)} custom-call(f32[4,16,896]{2,1,0:T(8,128)S(1)} %get-tuple-element.25.own_ref, bf16[4,16,896]{2,1,0:T(8,128)(2,1)S(1)} %collective-permute-done.3.near_a, bf16[4,16,896]{2,1,0:T(8,128)(2,1)S(1)} %collective-permute-done.4.near_b, bf16[4,16,896]{2,1,0:T(8,128)(2,1)S(1)} %collective-permute-done.5.near_c, ...), custom_call_target="tpu_custom_call" | custom-call | flops 500000 | bytes 1000000 | tf_op jit(solution)/shard_map/pallas_call | solution.py:227
  79.1 0.0 all-to-all-done.2.back_ref
  79.1 4.9 %all-to-all-start.3 = ((bf16[4,16,1024]{2,1,0:T(8,128)(2,1)}), bf16[4,16,1024]{2,1,0:T(8,128)(2,1)S(1)}, u32[]{:S(2)}, u32[]{:S(2)}) async-start(bf16[4,16,1024]{2,1,0:T(8,128)(2,1)} %shard_map.62), calls=%async_computation.3 | async-start | bytes 262144 | tf_op jit(solution)/shard_map/all_to_all | solution.py:308
  84.0 0.9 shard_map.64
  84.9 15.5 %all-to-all-done.3.back_ref = bf16[4,16,1024]{2,1,0:T(8,128)(2,1)S(1)} async-done(((bf16[4,16,1024]{2,1,0:T(8,128)(2,1)}), bf16[4,16,1024]{2,1,0:T(8,128)(2,1)S(1)}, u32[]{:S(2)}, u32[]{:S(2)}) %all-to-all-start.3) | async-done | bytes 131104 | tf_op jit(solution)/shard_map/all_to_all | solution.py:308
  100.5 0.9 shard_map.65
Async XLA Ops:
  0.6 0.8 copy-start
  2.2 14.3 %copy-start.1 = (bf16[12,1152]{1,0:T(8,128)(2,1)S(1)}, bf16[12,1152]{1,0:T(8,128)(2,1)}, u32[]{:S(2)}) copy-start(bf16[12,1152]{1,0:T(8,128)(2,1)} %emb_ref.2) | copy-start | bytes 82948
  2.2 30.0 %all-to-all-start = ((bf16[4,16,896]{2,1,0:T(8,128)(2,1)}), bf16[4,16,896]{2,1,0:T(8,128)(2,1)S(1)}, u32[]{:S(2)}, u32[]{:S(2)}) async-start(bf16[4,16,896]{2,1,0:T(8,128)(2,1)} %get-tuple-element.22), calls=%async_computation | async-start | bytes 229376 | tf_op jit(solution)/shard_map/all_to_all | solution.py:298
  32.2 23.0 %all-to-all-start.1 = ((bf16[32,16,896]{2,1,0:T(8,128)(2,1)}), bf16[32,16,896]{2,1,0:T(8,128)(2,1)S(1)}, u32[]{:S(2)}, u32[]{:S(2)}) async-start(bf16[32,16,896]{2,1,0:T(8,128)(2,1)} %get-tuple-element.23), calls=%async_computation.1 | async-start | bytes 1835008 | tf_op jit(solution)/shard_map/all_to_all | solution.py:301
  39.5 9.2 %collective-permute-start.2 = (bf16[4,16,896]{2,1,0:T(8,128)(2,1)S(1)}, bf16[4,16,896]{2,1,0:T(8,128)(2,1)S(1)}, u32[]{:S(2)}, u32[]{:S(2)}) collective-permute-start(bf16[4,16,896]{2,1,0:T(8,128)(2,1)S(1)} %all-to-all-done.refs_0_), channel_id=1, source_target_pairs={{0,32},{16,116},{32,64},{48,16},{64,96},{80,48},{96,4},{112,80},{4... | collective-permute-start | bytes 344072 | tf_op jit(solution)/shard_map/ppermute | solution.py:284
  41.5 8.6 %collective-permute-start.1 = (bf16[4,16,896]{2,1,0:T(8,128)(2,1)S(1)}, bf16[4,16,896]{2,1,0:T(8,128)(2,1)S(1)}, u32[]{:S(2)}, u32[]{:S(2)}) collective-permute-start(bf16[4,16,896]{2,1,0:T(8,128)(2,1)S(1)} %all-to-all-done.refs_0_), channel_id=1, source_target_pairs={{0,116},{16,0},{32,16},{48,32},{64,48},{80,64},{96,80},{112,96},{4... | collective-permute-start | bytes 344072 | tf_op jit(solution)/shard_map/ppermute | solution.py:284
  45.2 6.7 %collective-permute-start = (bf16[4,16,896]{2,1,0:T(8,128)(2,1)S(1)}, bf16[4,16,896]{2,1,0:T(8,128)(2,1)S(1)}, u32[]{:S(2)}, u32[]{:S(2)}) collective-permute-start(bf16[4,16,896]{2,1,0:T(8,128)(2,1)S(1)} %all-to-all-done.refs_0_), channel_id=1, source_target_pairs={{0,16},{16,32},{32,48},{48,64},{64,80},{80,96},{96,112},{112,4},{4... | collective-permute-start | bytes 344072 | tf_op jit(solution)/shard_map/ppermute | solution.py:284
  59.2 19.9 %all-to-all-start.2 = ((bf16[32,16,896]{2,1,0:T(8,128)(2,1)}), bf16[32,16,896]{2,1,0:T(8,128)(2,1)S(1)}, u32[]{:S(2)}, u32[]{:S(2)}) async-start(bf16[32,16,896]{2,1,0:T(8,128)(2,1)} %shard_map.63), calls=%async_computation.2 | async-start | bytes 1835008 | tf_op jit(solution)/shard_map/all_to_all | solution.py:305
  63.3 10.3 %collective-permute-start.3 = (bf16[4,16,896]{2,1,0:T(8,128)(2,1)S(1)}, bf16[4,16,896]{2,1,0:T(8,128)(2,1)S(1)}, u32[]{:S(2)}, u32[]{:S(2)}) collective-permute-start(bf16[4,16,896]{2,1,0:T(8,128)(2,1)S(1)} %get-tuple-element.26), channel_id=1, source_target_pairs={{0,116},{16,0},{32,16},{48,32},{64,48},{80,64},{96,80},{112,96},{4... | collective-permute-start | bytes 344072 | tf_op jit(solution)/shard_map/ppermute | solution.py:284
  66.5 7.0 %collective-permute-start.4 = (bf16[4,16,896]{2,1,0:T(8,128)(2,1)S(1)}, bf16[4,16,896]{2,1,0:T(8,128)(2,1)S(1)}, u32[]{:S(2)}, u32[]{:S(2)}) collective-permute-start(bf16[4,16,896]{2,1,0:T(8,128)(2,1)S(1)} %get-tuple-element.27), channel_id=1, source_target_pairs={{0,16},{16,32},{32,48},{48,64},{64,80},{80,96},{96,112},{112,4},{4... | collective-permute-start | bytes 344072 | tf_op jit(solution)/shard_map/ppermute | solution.py:284
  69.1 8.7 %collective-permute-start.5 = (bf16[4,16,896]{2,1,0:T(8,128)(2,1)S(1)}, bf16[4,16,896]{2,1,0:T(8,128)(2,1)S(1)}, u32[]{:S(2)}, u32[]{:S(2)}) collective-permute-start(bf16[4,16,896]{2,1,0:T(8,128)(2,1)S(1)} %get-tuple-element.28), channel_id=1, source_target_pairs={{0,32},{16,116},{32,64},{48,16},{64,96},{80,48},{96,4},{112,80},{4... | collective-permute-start | bytes 344072 | tf_op jit(solution)/shard_map/ppermute | solution.py:284
  79.1 21.3 %all-to-all-start.3 = ((bf16[4,16,1024]{2,1,0:T(8,128)(2,1)}), bf16[4,16,1024]{2,1,0:T(8,128)(2,1)S(1)}, u32[]{:S(2)}, u32[]{:S(2)}) async-start(bf16[4,16,1024]{2,1,0:T(8,128)(2,1)} %shard_map.62), calls=%async_computation.3 | async-start | bytes 262144 | tf_op jit(solution)/shard_map/all_to_all | solution.py:308
where the time goes:
time: 102 us; the launch traced here: 101 us
  starting transfers between devices  48.6 us (48%)
  waiting for transfers between devices  40.9 us (40%)
  Pallas kernels  8.94 us (9%)
  between operations  2.04 us (2%)
    ppermute x6, starting transfers between devices, along_z(): lax.ppermute(value, LINE, [(spot(z), spot(move(z) % 16)) for z in range(1...  18 us
    all_to_all x1, waiting for transfers between devices, on_device(): text_back = lax.all_to_all(message, FAR, 0, 0)  15.5 us
    all_to_all x1, waiting for transfers between devices, on_device(): own = lax.all_to_all(own, FAR, 0, 0)  14.6 us
    all_to_all x1, starting transfers between devices, on_device(): own = lax.all_to_all(own, FAR, 0, 0)  14.3 us
    ppermute x6, waiting for transfers between devices, along_z(): lax.ppermute(value, LINE, [(spot(z), spot(move(z) % 16)) for z in range(1...  7.45 us
    all_to_all x1, starting transfers between devices, on_device(): images = lax.all_to_all(sent, PLANE, 0, 0)  7.32 us
    all_to_all x1, starting transfers between devices, on_device(): text_back = lax.all_to_all(message, FAR, 0, 0)  4.9 us
    all_to_all x1, starting transfers between devices, on_device(): image_back = lax.all_to_all(image_terms(coeff, whole), PLANE, 0, 0)  4.05 us
  transfers between devices with their start and end apart: 10, of which 6 were waited for; matrix products, arithmetic and copies ran while one was open for 0% of the time, Pallas kernels for 3%

commit v1 on v0

--- a/solution.py
+++ b/solution.py
@@ -8,7 +8,7 @@
 EPS = 1e-06
 AXES = ("x", "zm", "zn", "core", "zh", "y")
 SIZES = (4, 2, 4, 2, 2, 4)
-PLANE = ("x", "core", "y")
+PLANE = ("x", "y")
 LINE = ("zm", "zn", "zh")
 FAR = ("zm", "zh")
 VMEM = 48 * 1024 * 1024
@@ -291,23 +291,35 @@
 )
 
 
+def across(value):
+    return lax.ppermute(value, "core", [(0, 1), (1, 0)])
+
+
 def on_device(image_embeds, text_embeds, log_temp, bias):
-    place = jnp.stack([lax.axis_index(PLANE), lax.axis_index(FAR)]).astype(jnp.int32)
+    place = jnp.stack([2 * lax.axis_index(PLANE), lax.axis_index(FAR)]).astype(jnp.int32)
+    chips = lax.axis_size(PLANE)
 
     own, txt_unit, txt_inv, txt_half = spread(text_embeds, lax.axis_size(FAR))
     own = lax.all_to_all(own, FAR, 0, 0)
-    sent, img_unit, img_inv, _ = spread(image_embeds, lax.axis_size(PLANE))
+    sent, img_unit, img_inv, _ = spread(image_embeds, 1)
+    sent = jnp.concatenate([sent, across(sent)], axis=0)
+    sent = jnp.broadcast_to(sent[None], (chips,) + sent.shape)
     sent, own = lax.optimization_barrier((sent, own))
-    images = lax.all_to_all(sent, PLANE, 0, 0)
+    images = lax.all_to_all(sent, PLANE, 0, 0).reshape((2 * chips,) + sent.shape[2:])
     texts = [own] + [along_z(own, there) for there, _ in NEAR]
 
     coeff, whole, part, *near_parts = text_terms(log_temp, bias, place, images, texts)
-    image_back = lax.all_to_all(image_terms(coeff, whole), PLANE, 0, 0)
+    image_part = image_terms(coeff, whole)
+    image_back = lax.all_to_all(
+        image_part.reshape((chips, 2) + image_part.shape[1:]), PLANE, 0, 0
+    )
     near = [along_z(near_part, home) for near_part, (_, home) in zip(near_parts, NEAR)]
     message, image_back = lax.optimization_barrier((far_message(part, near, whole), image_back))
     text_back = lax.all_to_all(message, FAR, 0, 0)
+    image_sum = jnp.sum(image_back.astype(jnp.float32), axis=0)
+    image_sum = jnp.stack([image_sum[0], across(image_sum[1])], axis=0)
     return (
-        finish(finish_images_kernel, img_unit, img_inv, image_back),
+        finish(finish_images_kernel, img_unit, img_inv, image_sum),
         finish(finish_texts_kernel, txt_unit, txt_inv, txt_half, text_back),
     )
 

time: 102 us -> 103 us (level)
  the two profiles are of different devices: /device:TPU:32 before, /device:TPU:2 now
where the time goes in v1:
time: 103 us; the launch traced here: 102 us
  starting transfers between devices  59.1 us (57%)
  waiting for transfers between devices  29.6 us (29%)
  Pallas kernels  8.37 us (8%)
  local copies, waits for them, and re-layouts  2.53 us (2%)
  between operations  2.04 us (2%)
    ppermute x6, starting transfers between devices, along_z(): lax.ppermute(value, LINE, [(spot(z), spot(move(z) % 16)) for z in range(1...  19 us
    all_to_all x1, starting transfers between devices, on_device(): own = lax.all_to_all(own, FAR, 0, 0)  15.1 us
    all_to_all x1, waiting for transfers between devices, on_device(): text_back = lax.all_to_all(message, FAR, 0, 0)  9.29 us
    all_to_all x1, waiting for transfers between devices, on_device(): own = lax.all_to_all(own, FAR, 0, 0)  9.15 us
    ppermute x6, waiting for transfers between devices, along_z(): lax.ppermute(value, LINE, [(spot(z), spot(move(z) % 16)) for z in range(1...  8.79 us
    all_to_all x1, starting transfers between devices, on_device(): lax.all_to_all(sent, PLANE, 0, 0).reshape((2 * chips,) + sent.shape[2:])  7.48 us
    all_to_all x1, starting transfers between devices, on_device(): lax.all_to_all(image_part.reshape((chips, 2) + image_part.shape[1:]), PLA...  7.23 us
    all_to_all x1, starting transfers between devices, on_device(): text_back = lax.all_to_all(message, FAR, 0, 0)  6.47 us
  transfers between devices with their start and end apart: 12, of which 7 were waited for; matrix products, arithmetic and copies ran while one was open for 0% of the time, Pallas kernels for 3%

profile of v1, /device:TPU:2, one launch (start us, length us, event | category | flops | bytes accessed | tf_op | source)
XLA Modules:
  0.0 101.8 jit_solution(6220993129041689982)
XLA Ops:
  0.6 0.0 copy-start
  0.6 0.8 copy-done
  1.4 0.8 shard_map.60
  2.2 15.1 %all-to-all-start = ((bf16[4,16,896]{2,1,0:T(8,128)(2,1)}), bf16[4,16,896]{2,1,0:T(8,128)(2,1)S(1)}, u32[]{:S(2)}, u32[]{:S(2)}) async-start(bf16[4,16,896]{2,1,0:T(8,128)(2,1)} %get-tuple-element.22), calls=%async_computation | async-start | bytes 229376 | tf_op jit(solution)/shard_map/all_to_all | solution.py:303
  17.3 0.0 copy-start.1
  17.3 0.8 copy-done.1
  18.0 0.7 shard_map.59
  18.8 1.9 %collective-permute-start = (bf16[1,16,896]{2,1,0:T(8,128)(2,1)S(1)}, bf16[1,16,896]{2,1,0:T(8,128)(2,1)S(1)}, u32[]{:S(2)}, u32[]{:S(2)}) collective-permute-start(bf16[1,16,896]{2,1,0:T(8,128)(2,1)S(1)} %get-tuple-element.21), channel_id=1, source_target_pairs={{0,8},{8,0},{1,9},{9,1},{2,10},{10,2},{3,11},{11,3},{4,12},{12,4},... | collective-permute-start | bytes 86024 | tf_op jit(solution)/shard_map/ppermute | solution.py:295
  20.7 1.2 %collective-permute-done = bf16[1,16,896]{2,1,0:T(8,128)(2,1)S(1)} collective-permute-done((bf16[1,16,896]{2,1,0:T(8,128)(2,1)S(1)}, bf16[1,16,896]{2,1,0:T(8,128)(2,1)S(1)}, u32[]{:S(2)}, u32[]{:S(2)}) %collective-permute-start) | collective-permute-done | bytes 28704 | tf_op jit(solution)/shard_map/ppermute | solution.py:295
  21.9 9.1 %all-to-all-done.refs_0_ = bf16[4,16,896]{2,1,0:T(8,128)(2,1)S(1)} async-done(((bf16[4,16,896]{2,1,0:T(8,128)(2,1)}), bf16[4,16,896]{2,1,0:T(8,128)(2,1)S(1)}, u32[]{:S(2)}, u32[]{:S(2)}) %all-to-all-start) | async-done | bytes 114720 | tf_op jit(solution)/shard_map/all_to_all | solution.py:303
  31.0 1.0 broadcast_in_dim.2
  32.0 7.5 %all-to-all-start.1 = ((bf16[16,2,16,896]{3,2,1,0:T(8,128)(2,1)}), bf16[16,2,16,896]{3,2,1,0:T(8,128)(2,1)S(1)}, u32[]{:S(2)}, u32[]{:S(2)}) async-start(bf16[16,2,16,896]{3,2,1,0:T(8,128)(2,1)} %broadcast_in_dim.2), calls=%async_computation.1 | async-start | bytes 1835008 | tf_op jit(solution)/shard_map/all_to_all | solution.py:308
  39.5 4.7 %collective-permute-start.3 = (bf16[4,16,896]{2,1,0:T(8,128)(2,1)S(1)}, bf16[4,16,896]{2,1,0:T(8,128)(2,1)S(1)}, u32[]{:S(2)}, u32[]{:S(2)}) collective-permute-start(bf16[4,16,896]{2,1,0:T(8,128)(2,1)S(1)} %all-to-all-done.refs_0_), channel_id=1, source_target_pairs={{0,32},{16,116},{32,64},{48,16},{64,96},{80,48},{96,4},{112,80},{4... | collective-permute-start | bytes 344072 | tf_op jit(solution)/shard_map/ppermute | solution.py:284
  44.2 1.9 %collective-permute-start.2 = (bf16[4,16,896]{2,1,0:T(8,128)(2,1)S(1)}, bf16[4,16,896]{2,1,0:T(8,128)(2,1)S(1)}, u32[]{:S(2)}, u32[]{:S(2)}) collective-permute-start(bf16[4,16,896]{2,1,0:T(8,128)(2,1)S(1)} %all-to-all-done.refs_0_), channel_id=1, source_target_pairs={{0,116},{16,0},{32,16},{48,32},{64,48},{80,64},{96,80},{112,96},{4... | collective-permute-start | bytes 344072 | tf_op jit(solution)/shard_map/ppermute | solution.py:284
  46.1 3.9 %collective-permute-start.1 = (bf16[4,16,896]{2,1,0:T(8,128)(2,1)S(1)}, bf16[4,16,896]{2,1,0:T(8,128)(2,1)S(1)}, u32[]{:S(2)}, u32[]{:S(2)}) collective-permute-start(bf16[4,16,896]{2,1,0:T(8,128)(2,1)S(1)} %all-to-all-done.refs_0_), channel_id=1, source_target_pairs={{0,16},{16,32},{32,48},{48,64},{64,80},{80,96},{96,112},{112,4},{4... | collective-permute-start | bytes 344072 | tf_op jit(solution)/shard_map/ppermute | solution.py:284
  51.4 0.1 pad_add_fusion.place_ref
  51.4 0.0 collective-permute-done.3.refs_3_
  51.4 0.0 collective-permute-done.2.refs_2_
  51.4 2.6 %collective-permute-done.1.refs_1_ = bf16[4,16,896]{2,1,0:T(8,128)(2,1)S(1)} collective-permute-done((bf16[4,16,896]{2,1,0:T(8,128)(2,1)S(1)}, bf16[4,16,896]{2,1,0:T(8,128)(2,1)S(1)}, u32[]{:S(2)}, u32[]{:S(2)}) %collective-permute-start.1) | collective-permute-done | bytes 114720 | tf_op jit(solution)/shard_map/ppermute | solution.py:284
  54.0 0.0 all-to-all-done.1
  54.0 2.4 %shard_map.61 = (bf16[512,256]{1,0:T(8,128)(2,1)S(1)}, bf16[256,1152]{1,0:T(8,128)(2,1)S(1)}, f32[4,16,896]{2,1,0:T(8,128)S(1)}, bf16[4,16,896]{2,1,0:T(8,128)(2...) custom-call(f32[1]{0:T(128)S(6)} %copy.6.temp_ref, f32[1]{0:T(128)S(6)} %copy.7.bias_ref, ...), custom_call_target="tpu_custom_call" | custom-call | flops 600000000 | bytes 4000000 | tf_op jit(solution)/shard_map/pallas_call | solution.py:120
  56.5 1.5 %shard_map.63 = bf16[32,16,896]{2,1,0:T(8,128)(2,1)} custom-call(bf16[512,256]{1,0:T(8,128)(2,1)S(1)} %get-tuple-element.30.coeff_ref, bf16[256,1152]{1,0:T(8,128)(2,1)S(1)} %get-tuple-element.29.half_ref.texts_ref), custom_call_target="tpu_custom_call" | custom-call | flops 300000000 | bytes 2000000 | tf_op jit(solution)/shard_map/pallas_call | solution.py:156
  58.0 7.2 %all-to-all-start.2 = ((bf16[16,2,16,896]{3,2,1,0:T(8,128)(2,1)}), bf16[16,2,16,896]{3,2,1,0:T(8,128)(2,1)S(1)}, u32[]{:S(2)}, u32[]{:S(2)}) async-start(bf16[16,2,16,896]{3,2,1,0:T(8,128)(2,1)} %bitcast.3), calls=%async_computation.2 | async-start | bytes 1835008 | tf_op jit(solution)/shard_map/all_to_all | solution.py:313
  65.2 2.6 %collective-permute-start.4 = (bf16[4,16,896]{2,1,0:T(8,128)(2,1)S(1)}, bf16[4,16,896]{2,1,0:T(8,128)(2,1)S(1)}, u32[]{:S(2)}, u32[]{:S(2)}) collective-permute-start(bf16[4,16,896]{2,1,0:T(8,128)(2,1)S(1)} %get-tuple-element.26), channel_id=1, source_target_pairs={{0,116},{16,0},{32,16},{48,32},{64,48},{80,64},{96,80},{112,96},{4... | collective-permute-start | bytes 344072 | tf_op jit(solution)/shard_map/ppermute | solution.py:284
  67.8 3.3 %collective-permute-start.5 = (bf16[4,16,896]{2,1,0:T(8,128)(2,1)S(1)}, bf16[4,16,896]{2,1,0:T(8,128)(2,1)S(1)}, u32[]{:S(2)}, u32[]{:S(2)}) collective-permute-start(bf16[4,16,896]{2,1,0:T(8,128)(2,1)S(1)} %get-tuple-element.27), channel_id=1, source_target_pairs={{0,16},{16,32},{32,48},{48,64},{64,80},{80,96},{96,112},{112,4},{4... | collective-permute-start | bytes 344072 | tf_op jit(solution)/shard_map/ppermute | solution.py:284
  71.1 2.6 %collective-permute-start.6 = (bf16[4,16,896]{2,1,0:T(8,128)(2,1)S(1)}, bf16[4,16,896]{2,1,0:T(8,128)(2,1)S(1)}, u32[]{:S(2)}, u32[]{:S(2)}) collective-permute-start(bf16[4,16,896]{2,1,0:T(8,128)(2,1)S(1)} %get-tuple-element.28), channel_id=1, source_target_pairs={{0,32},{16,116},{32,64},{48,16},{64,96},{80,48},{96,4},{112,80},{4... | collective-permute-start | bytes 344072 | tf_op jit(solution)/shard_map/ppermute | solution.py:284
  73.7 0.0 collective-permute-done.4.near_a
  73.7 2.7 %collective-permute-done.5.near_b = bf16[4,16,896]{2,1,0:T(8,128)(2,1)S(1)} collective-permute-done((bf16[4,16,896]{2,1,0:T(8,128)(2,1)S(1)}, bf16[4,16,896]{2,1,0:T(8,128)(2,1)S(1)}, u32[]{:S(2)}, u32[]{:S(2)}) %collective-permute-start.5) | collective-permute-done | bytes 114720 | tf_op jit(solution)/shard_map/ppermute | solution.py:284
  76.4 3.5 %collective-permute-done.6.near_c = bf16[4,16,896]{2,1,0:T(8,128)(2,1)S(1)} collective-permute-done((bf16[4,16,896]{2,1,0:T(8,128)(2,1)S(1)}, bf16[4,16,896]{2,1,0:T(8,128)(2,1)S(1)}, u32[]{:S(2)}, u32[]{:S(2)}) %collective-permute-start.6) | collective-permute-done | bytes 114720 | tf_op jit(solution)/shard_map/ppermute | solution.py:284
  79.9 1.3 %shard_map.62 = bf16[4,16,1024]{2,1,0:T(8,128)(2,1)} custom-call(f32[4,16,896]{2,1,0:T(8,128)S(1)} %get-tuple-element.25.own_ref, bf16[4,16,896]{2,1,0:T(8,128)(2,1)S(1)} %collective-permute-done.4.near_a, bf16[4,16,896]{2,1,0:T(8,128)(2,1)S(1)} %collective-permute-done.5.near_b, bf16[4,16,896]{2,1,0:T(8,128)(2,1)S(1)} %collective-permute-done.6.near_c, ...), custom_call_target="tpu_custom_call" | custom-call | flops 500000 | bytes 1000000 | tf_op jit(solution)/shard_map/pallas_call | solution.py:227
  81.1 0.0 all-to-all-done.2
  81.1 0.1 convert_reduce_fusion
  81.3 6.5 %all-to-all-start.3 = ((bf16[4,16,1024]{2,1,0:T(8,128)(2,1)}), bf16[4,16,1024]{2,1,0:T(8,128)(2,1)S(1)}, u32[]{:S(2)}, u32[]{:S(2)}) async-start(bf16[4,16,1024]{2,1,0:T(8,128)(2,1)} %shard_map.62), calls=%async_computation.3 | async-start | bytes 262144 | tf_op jit(solution)/shard_map/all_to_all | solution.py:318
  87.7 1.9 %collective-permute-start.7 = (f32[16,896]{1,0:T(8,128)S(1)}, f32[16,896]{1,0:T(8,128)S(1)}, u32[]{:S(2)}, u32[]{:S(2)}) collective-permute-start(f32[16,896]{1,0:T(8,128)S(1)} %get-tuple-element.37), channel_id=1, source_target_pairs={{0,8},{8,0},{1,9},{9,1},{2,10},{10,2},{3,11},{11,3},{4,12},{12,4},... | collective-permute-start | bytes 172040 | tf_op jit(solution)/shard_map/ppermute | solution.py:295
  89.7 1.2 %collective-permute-done.7 = f32[16,896]{1,0:T(8,128)S(1)} collective-permute-done((f32[16,896]{1,0:T(8,128)S(1)}, f32[16,896]{1,0:T(8,128)S(1)}, u32[]{:S(2)}, u32[]{:S(2)}) %collective-permute-start.7) | collective-permute-done | bytes 57376 | tf_op jit(solution)/shard_map/ppermute | solution.py:295
  90.9 0.7 shard_map.64
  91.6 9.3 %all-to-all-done.3.back_ref = bf16[4,16,1024]{2,1,0:T(8,128)(2,1)S(1)} async-done(((bf16[4,16,1024]{2,1,0:T(8,128)(2,1)}), bf16[4,16,1024]{2,1,0:T(8,128)(2,1)S(1)}, u32[]{:S(2)}, u32[]{:S(2)}) %all-to-all-start.3) | async-done | bytes 131104 | tf_op jit(solution)/shard_map/all_to_all | solution.py:318
  100.9 0.9 shard_map.65
  (3 shorter events, 0.0 us)
Async XLA Ops:
  0.6 0.8 copy-start
  2.2 28.8 %all-to-all-start = ((bf16[4,16,896]{2,1,0:T(8,128)(2,1)}), bf16[4,16,896]{2,1,0:T(8,128)(2,1)S(1)}, u32[]{:S(2)}, u32[]{:S(2)}) async-start(bf16[4,16,896]{2,1,0:T(8,128)(2,1)} %get-tuple-element.22), calls=%async_computation | async-start | bytes 229376 | tf_op jit(solution)/shard_map/all_to_all | solution.py:303
  17.3 0.8 copy-start.1
  18.8 3.1 %collective-permute-start = (bf16[1,16,896]{2,1,0:T(8,128)(2,1)S(1)}, bf16[1,16,896]{2,1,0:T(8,128)(2,1)S(1)}, u32[]{:S(2)}, u32[]{:S(2)}) collective-permute-start(bf16[1,16,896]{2,1,0:T(8,128)(2,1)S(1)} %get-tuple-element.21), channel_id=1, source_target_pairs={{0,8},{8,0},{1,9},{9,1},{2,10},{10,2},{3,11},{11,3},{4,12},{12,4},... | collective-permute-start | bytes 86024 | tf_op jit(solution)/shard_map/ppermute | solution.py:295
  32.0 22.0 %all-to-all-start.1 = ((bf16[16,2,16,896]{3,2,1,0:T(8,128)(2,1)}), bf16[16,2,16,896]{3,2,1,0:T(8,128)(2,1)S(1)}, u32[]{:S(2)}, u32[]{:S(2)}) async-start(bf16[16,2,16,896]{3,2,1,0:T(8,128)(2,1)} %broadcast_in_dim.2), calls=%async_computation.1 | async-start | bytes 1835008 | tf_op jit(solution)/shard_map/all_to_all | solution.py:308
  39.5 12.0 %collective-permute-start.3 = (bf16[4,16,896]{2,1,0:T(8,128)(2,1)S(1)}, bf16[4,16,896]{2,1,0:T(8,128)(2,1)S(1)}, u32[]{:S(2)}, u32[]{:S(2)}) collective-permute-start(bf16[4,16,896]{2,1,0:T(8,128)(2,1)S(1)} %all-to-all-done.refs_0_), channel_id=1, source_target_pairs={{0,32},{16,116},{32,64},{48,16},{64,96},{80,48},{96,4},{112,80},{4... | collective-permute-start | bytes 344072 | tf_op jit(solution)/shard_map/ppermute | solution.py:284
  44.2 7.2 %collective-permute-start.2 = (bf16[4,16,896]{2,1,0:T(8,128)(2,1)S(1)}, bf16[4,16,896]{2,1,0:T(8,128)(2,1)S(1)}, u32[]{:S(2)}, u32[]{:S(2)}) collective-permute-start(bf16[4,16,896]{2,1,0:T(8,128)(2,1)S(1)} %all-to-all-done.refs_0_), channel_id=1, source_target_pairs={{0,116},{16,0},{32,16},{48,32},{64,48},{80,64},{96,80},{112,96},{4... | collective-permute-start | bytes 344072 | tf_op jit(solution)/shard_map/ppermute | solution.py:284
  46.1 7.9 %collective-permute-start.1 = (bf16[4,16,896]{2,1,0:T(8,128)(2,1)S(1)}, bf16[4,16,896]{2,1,0:T(8,128)(2,1)S(1)}, u32[]{:S(2)}, u32[]{:S(2)}) collective-permute-start(bf16[4,16,896]{2,1,0:T(8,128)(2,1)S(1)} %all-to-all-done.refs_0_), channel_id=1, source_target_pairs={{0,16},{16,32},{32,48},{48,64},{64,80},{80,96},{96,112},{112,4},{4... | collective-permute-start | bytes 344072 | tf_op jit(solution)/shard_map/ppermute | solution.py:284
  58.0 23.1 %all-to-all-start.2 = ((bf16[16,2,16,896]{3,2,1,0:T(8,128)(2,1)}), bf16[16,2,16,896]{3,2,1,0:T(8,128)(2,1)S(1)}, u32[]{:S(2)}, u32[]{:S(2)}) async-start(bf16[16,2,16,896]{3,2,1,0:T(8,128)(2,1)} %bitcast.3), calls=%async_computation.2 | async-start | bytes 1835008 | tf_op jit(solution)/shard_map/all_to_all | solution.py:313
  65.2 8.4 %collective-permute-start.4 = (bf16[4,16,896]{2,1,0:T(8,128)(2,1)S(1)}, bf16[4,16,896]{2,1,0:T(8,128)(2,1)S(1)}, u32[]{:S(2)}, u32[]{:S(2)}) collective-permute-start(bf16[4,16,896]{2,1,0:T(8,128)(2,1)S(1)} %get-tuple-element.26), channel_id=1, source_target_pairs={{0,116},{16,0},{32,16},{48,32},{64,48},{80,64},{96,80},{112,96},{4... | collective-permute-start | bytes 344072 | tf_op jit(solution)/shard_map/ppermute | solution.py:284
  67.8 8.6 %collective-permute-start.5 = (bf16[4,16,896]{2,1,0:T(8,128)(2,1)S(1)}, bf16[4,16,896]{2,1,0:T(8,128)(2,1)S(1)}, u32[]{:S(2)}, u32[]{:S(2)}) collective-permute-start(bf16[4,16,896]{2,1,0:T(8,128)(2,1)S(1)} %get-tuple-element.27), channel_id=1, source_target_pairs={{0,16},{16,32},{32,48},{48,64},{64,80},{80,96},{96,112},{112,4},{4... | collective-permute-start | bytes 344072 | tf_op jit(solution)/shard_map/ppermute | solution.py:284
  71.1 8.8 %collective-permute-start.6 = (bf16[4,16,896]{2,1,0:T(8,128)(2,1)S(1)}, bf16[4,16,896]{2,1,0:T(8,128)(2,1)S(1)}, u32[]{:S(2)}, u32[]{:S(2)}) collective-permute-start(bf16[4,16,896]{2,1,0:T(8,128)(2,1)S(1)} %get-tuple-element.28), channel_id=1, source_target_pairs={{0,32},{16,116},{32,64},{48,16},{64,96},{80,48},{96,4},{112,80},{4... | collective-permute-start | bytes 344072 | tf_op jit(solution)/shard_map/ppermute | solution.py:284
  81.3 19.7 %all-to-all-start.3 = ((bf16[4,16,1024]{2,1,0:T(8,128)(2,1)}), bf16[4,16,1024]{2,1,0:T(8,128)(2,1)S(1)}, u32[]{:S(2)}, u32[]{:S(2)}) async-start(bf16[4,16,1024]{2,1,0:T(8,128)(2,1)} %shard_map.62), calls=%async_computation.3 | async-start | bytes 262144 | tf_op jit(solution)/shard_map/all_to_all | solution.py:318
  87.7 3.1 %collective-permute-start.7 = (f32[16,896]{1,0:T(8,128)S(1)}, f32[16,896]{1,0:T(8,128)S(1)}, u32[]{:S(2)}, u32[]{:S(2)}) collective-permute-start(f32[16,896]{1,0:T(8,128)S(1)} %get-tuple-element.37), channel_id=1, source_target_pairs={{0,8},{8,0},{1,9},{9,1},{2,10},{10,2},{3,11},{11,3},{4,12},{12,4},... | collective-permute-start | bytes 172040 | tf_op jit(solution)/shard_map/ppermute | solution.py:295
